TPU v7x, 512 devices: a whole 4x8x8 slice. The times are simulated.
512 devices in a mesh: along: 64 (over x, y, core), across: 8 (over z).
Axes of the slice: x: 4, y: 8, z: 8, core: 2. Of those that a mesh axis runs over, the one named last changes fastest.
Arguments:
- frames: bfloat16 [64, 3, 528, 2048], P('along', None, None, 'across'), may hold values from -6 to 6
- col_start: int32 [64, 8192], P('along', 'across'), may hold values from 0 to 252
- col_weights: bfloat16 [64, 4, 8192], P('along', None, 'across'), may hold values from 0.19921875 to 0.796875
- footprint: int32 [64, 33], P('along'), may hold values from 0 to 63, as said below
- row_start: int32 [64, 33, 8], P('along'), may hold values from 0 to 12
- row_weights: bfloat16 [64, 33, 4, 8], P('along'), may hold values from 0.19921875 to 0.796875
- seg_weight: bfloat16 [64, 33], P('along'), may hold values from 0.19921875 to 5
- feather_width: int32 [64, 8], P('along', 'across'), may hold values from 1 to 4
Outputs:
- ortho_strip: bfloat16 [3, 512, 8192], P(None, 'along', 'across')
Inputs may be any that keep to these rules, and one draw needn't show every extreme that they name: footprint[f, s] = start_f + s: each frame covers 33 consecutive tiles in order, start_f never falls as f grows, start_f is 0 or f - 32 or one less, and every tile is named by some frame.
All inputs are finite; a program needn't handle non-finite values.
Results may differ from a plain program's by a relative error of at most 0.015.
Values may be sent and summed in bfloat16 or wider, within the bound.
A program may use at most 64 MiB of HBM per device.

v0:
```python
import jax
import jax.numpy as jnp
from jax import lax
from jax.sharding import PartitionSpec as P


def with_halo(block, sides, width):
    for axis, dim in sides:
        count = lax.axis_size(axis)
        forward = [(i, i + 1) for i in range(count - 1)]
        backward = [(target, source) for source, target in forward]
        low = lax.ppermute(
            lax.slice_in_dim(block, block.shape[dim] - width, None, axis=dim), axis, forward
        )
        high = lax.ppermute(lax.slice_in_dim(block, 0, width, axis=dim), axis, backward)
        block = jnp.concatenate([low, block, high], axis=dim)
    return block


def body(
    frames, col_start, col_weights, footprint, row_start, row_weights, seg_weight, feather_width
):
    channels = frames.shape[1]
    frame_rows = frames.shape[2]
    frame_cols = frames.shape[3]
    tile_cols = col_start.shape[1]
    band_size = col_weights.shape[1]
    seg_count = row_start.shape[1]
    tile_rows = row_start.shape[2]
    sub_rows = frame_rows // seg_count
    readers = lax.axis_size("along")
    frame_pos = jnp.arange(frame_cols, dtype=jnp.int32)
    col_offsets = frame_pos[:, None] - col_start[0][None, :]
    col_matrix = jnp.zeros((frame_cols, tile_cols), jnp.bfloat16)
    for step in range(band_size):
        col_matrix = jnp.where(col_offsets == step, col_weights[0, step][None, :], col_matrix)
    flat_frame = frames[0].reshape(channels * frame_rows, frame_cols)
    col_part = jnp.dot(flat_frame, col_matrix, preferred_element_type=jnp.float32).astype(
        jnp.bfloat16
    )
    col_part = col_part.reshape(channels, seg_count, sub_rows, tile_cols)
    seg_pos = jnp.arange(sub_rows, dtype=jnp.int32)
    row_offsets = seg_pos[None, None, :] - row_start[0][:, :, None]
    row_matrix = jnp.zeros((seg_count, tile_rows, sub_rows), jnp.bfloat16)
    for step in range(band_size):
        row_matrix = jnp.where(row_offsets == step, row_weights[0][:, step, :, None], row_matrix)
    routing = (footprint[0][None, :] == jnp.arange(readers, dtype=jnp.int32)[:, None]).astype(
        jnp.bfloat16
    )
    slot_weight = jnp.dot(routing, seg_weight[0], preferred_element_type=jnp.float32).astype(
        jnp.bfloat16
    )
    out_segments = jnp.einsum(
        "ns,csrt->ncrt", routing, col_part, preferred_element_type=jnp.float32
    ).astype(jnp.bfloat16)
    out_rows = jnp.einsum(
        "ns,sik->nik", routing, row_matrix, preferred_element_type=jnp.float32
    ).astype(jnp.bfloat16)
    got_segments, got_rows, arrived_weight = (
        lax.all_to_all(out_segments, "along", split_axis=0, concat_axis=0, tiled=True),
        lax.all_to_all(out_rows, "along", split_axis=0, concat_axis=0, tiled=True),
        lax.all_to_all(slot_weight, "along", split_axis=0, concat_axis=0, tiled=True),
    )
    arrived = jnp.einsum(
        "nik,nckt->ncit", got_rows, got_segments, preferred_element_type=jnp.float32
    ).astype(jnp.bfloat16)
    numerator = jnp.einsum(
        "n,ncit->cit", arrived_weight, arrived, preferred_element_type=jnp.float32
    )
    denominator = jnp.sum(arrived_weight.astype(jnp.float32))
    blended = (numerator / denominator).astype(jnp.bfloat16)
    padded = with_halo(blended, (("along", 1), ("across", 2)), 1)
    values = blended.astype(jnp.float32)
    up_row = padded[:, 0, 1:-1].astype(jnp.float32)
    down_row = padded[:, -1, 1:-1].astype(jnp.float32)
    left_col = padded[:, 1:-1, 0].astype(jnp.float32)
    right_col = padded[:, 1:-1, -1].astype(jnp.float32)
    along_index = lax.axis_index("along")
    across_index = lax.axis_index("across")
    has_up = (along_index > 0).astype(jnp.float32)
    has_down = (along_index < lax.axis_size("along") - 1).astype(jnp.float32)
    has_left = (across_index > 0).astype(jnp.float32)
    has_right = (across_index < lax.axis_size("across") - 1).astype(jnp.float32)
    width = feather_width[0, 0].astype(jnp.float32)
    row_pos = jnp.arange(tile_rows, dtype=jnp.float32)
    col_pos = jnp.arange(tile_cols, dtype=jnp.float32)
    ramp_top = jnp.maximum(0.0, 1.0 - row_pos / width)
    ramp_bottom = jnp.maximum(0.0, 1.0 - (tile_rows - 1 - row_pos) / width)
    ramp_left = jnp.maximum(0.0, 1.0 - col_pos / width)
    ramp_right = jnp.maximum(0.0, 1.0 - (tile_cols - 1 - col_pos) / width)
    diff_up = has_up * (up_row - values[:, 0, :])
    diff_down = has_down * (down_row - values[:, -1, :])
    diff_left = has_left * (left_col - values[:, :, 0])
    diff_right = has_right * (right_col - values[:, :, -1])
    result = values + 0.5 * ramp_top[None, :, None] * diff_up[:, None, :]
    result = result + 0.5 * ramp_bottom[None, :, None] * diff_down[:, None, :]
    side = (
        0.5 * ramp_left[None, None, :] * diff_left[:, :, None]
        + 0.5 * ramp_right[None, None, :] * diff_right[:, :, None]
    )
    result = result + side
    return result.astype(jnp.bfloat16)


def solution(mesh):
    placed = (
        P("along", None, None, "across"),
        P("along", "across"),
        P("along", None, "across"),
        P("along", None),
        P("along", None, None),
        P("along", None, None, None),
        P("along", None),
        P("along", "across"),
    )
    return jax.shard_map(
        body, mesh=mesh, in_specs=placed, out_specs=P(None, "along", "across"), check_vma=False
    )
```

profile of v0, /device:TPU:1, one launch (start us, length us, event | category | flops | bytes accessed | tf_op | source)
XLA Modules:
  0.0 220.2 jit_solution(14218911356432417835)
XLA Ops:
  0.0 0.0 copy-start
  0.0 0.9 fusion.8
  0.9 0.7 copy.27
  1.7 11.6 %all-to-all-start = ((bf16[64,1,1]{2,1,0:T(2,128)(2,1)}), bf16[64,1,1]{2,1,0:T(2,128)(2,1)S(1)}, u32[]{:S(2)}, u32[]{:S(2)}) async-start(bf16[64,1,1]{2,1,0:T(2,128)(2,1)} %copy.27), calls=%async_computation | async-start | bytes 65536 | tf_op jit(solution)/shard_map/all_to_all | solution.py:62
  13.3 0.9 slice_reduce_fusion.3
  14.2 0.7 slice_bitcast_fusion.3
  14.9 0.7 fusion.34
  15.7 0.0 copy-done
  15.7 0.0 copy-start.1
  15.7 3.5 %convolution_convert_fusion = bf16[1024,1584]{0,1:T(8,128)(2,1)} fusion(bf16[1584,256]{1,0:T(8,128)(2,1)S(1)} %bitcast.60, s32[1024]{0:T(1024)} %bitcast.69, bf16[1024]{0:T(1024)(128)(2,1)S(1)} %get-tuple-element.9, bf16[1024]{0:T(1024)(128)(2,1)S(1)} %get-tuple-element.10, bf16[1024]{0:T(1024)(128)(2,1)S(1)} %get-tuple-element.8, ...), kind=kOutput, calls=%fused_computation.2 | convolution fusion | flops 834453504 | bytes 4067328 | tf_op jit(solution)/shard_map/dot_general | solution.py:38
  19.2 0.0 copy-done.1
  19.2 0.2 fusion.38
  19.4 0.8 copy.30
  20.2 2.3 %all-to-all-done = bf16[64,1,1]{2,1,0:T(2,128)(2,1)S(1)} async-done(((bf16[64,1,1]{2,1,0:T(2,128)(2,1)}), bf16[64,1,1]{2,1,0:T(2,128)(2,1)S(1)}, u32[]{:S(2)}, u32[]{:S(2)}) %all-to-all-start) | async-done | bytes 160 | tf_op jit(solution)/shard_map/all_to_all | solution.py:62
  22.5 8.0 %all-to-all-start.2 = ((bf16[64,8,16]{2,1,0:T(8,128)(2,1)}), bf16[64,8,16]{2,1,0:T(8,128)(2,1)S(1)}, u32[]{:S(2)}, u32[]{:S(2)}) async-start(bf16[64,8,16]{2,1,0:T(8,128)(2,1)} %copy.30), calls=%async_computation.2 | async-start | bytes 262144 | tf_op jit(solution)/shard_map/all_to_all | solution.py:61
  30.5 7.3 %fusion.2 = bf16[64,3,16,1024]{3,0,2,1:T(8,128)(2,1)S(1)} fusion(bf16[3,33,16,1024]{3,2,1,0:T(8,128)(2,1)} %bitcast.61, s32[33]{0:T(128)S(1)} %bitcast.68), kind=kOutput, calls=%fused_computation.3 | convolution fusion | flops 210765888 | bytes 9535620 | tf_op jit(solution)/shard_map/ns,csrt->ncrt/dot_general | solution.py:53
  37.9 6.2 %copy.29 = bf16[64,3,16,1024]{3,2,1,0:T(8,128)(2,1)} copy(bf16[64,3,16,1024]{3,0,2,1:T(8,128)(2,1)S(1)} %fusion.2) | data formatting | bytes 12582912 | tf_op jit(solution)/shard_map/convert_element_type | solution.py:55
  44.0 0.0 all-to-all-done.2
  44.0 10.5 %all-to-all-start.1 = ((bf16[64,3,16,1024]{3,2,1,0:T(8,128)(2,1)}), bf16[64,3,16,1024]{3,2,1,0:T(8,128)(2,1)}, u32[]{:S(2)}, u32[]{:S(2)}) async-start(bf16[64,3,16,1024]{3,2,1,0:T(8,128)(2,1)} %copy.29), calls=%async_computation.1 | async-start | bytes 12582912 | tf_op jit(solution)/shard_map/all_to_all | solution.py:60
  55.2 0.6 reduce
  55.8 0.6 convert_reduce_fusion
  56.4 139.0 %all-to-all-done.1 = bf16[64,3,16,1024]{3,2,1,0:T(8,128)(2,1)} async-done(((bf16[64,3,16,1024]{3,2,1,0:T(8,128)(2,1)}), bf16[64,3,16,1024]{3,2,1,0:T(8,128)(2,1)}, u32[]{:S(2)}, u32[]{:S(2)}) %all-to-all-start.1) | async-done | bytes 6291488 | tf_op jit(solution)/shard_map/all_to_all | solution.py:60
  195.4 3.7 %convert_bitcast_fusion = bf16[64,3,8,1024]{3,2,1,0:T(8,128)(2,1)S(1)} fusion(bf16[64,3,16,1024]{3,2,1,0:T(8,128)(2,1)} %all-to-all-done.1, bf16[64,8,16]{2,1,0:T(8,128)(2,1)S(1)} %all-to-all-done.2), kind=kOutput, calls=%fused_computation.6 | convolution fusion | flops 51904512 | bytes 9453568 | tf_op jit(solution)/shard_map/nik,nckt->ncit/dot_general | solution.py:64
  199.1 3.4 %fusion.5 = f32[1,3,8,1024]{3,0,2,1:T(1,128)S(1)} fusion(bf16[64,3,8,1024]{3,2,1,0:T(8,128)(2,1)S(1)} %convert_bitcast_fusion, bf16[64]{0:T(256)(128)(2,1)S(1)} %reduce), kind=kOutput, calls=%fused_computation.4 | convolution fusion | flops 3145728 | bytes 3244160 | tf_op jit(solution)/shard_map/n,ncit->cit/dot_general | solution.py:67
  202.5 0.7 fusion.57
  203.2 1.9 collective-permute-start
  205.2 2.4 %collective-permute-start.1 = (bf16[3,1,1024]{2,1,0:T(2,128)(2,1)S(1)}, bf16[3,1,1024]{2,1,0:T(2,128)(2,1)S(1)}, u32[]{:S(2)}, u32[]{:S(2)}) collective-permute-start(bf16[3,1,1024]{2,1,0:T(2,128)(2,1)S(1)} %get-tuple-element.18), channel_id=1, source_target_pairs={{8,0},{16,8},{24,16},{32,24},{40,32},{48,40},{56,48},{64,56},{72,6... | collective-permute-start | bytes 18440 | tf_op jit(solution)/shard_map/ppermute | solution.py:15
  207.6 0.0 collective-permute-done
  207.6 2.6 %collective-permute-done.1 = bf16[3,1,1024]{2,1,0:T(2,128)(2,1)S(1)} collective-permute-done((bf16[3,1,1024]{2,1,0:T(2,128)(2,1)S(1)}, bf16[3,1,1024]{2,1,0:T(2,128)(2,1)S(1)}, u32[]{:S(2)}, u32[]{:S(2)}) %collective-permute-start.1) | collective-permute-done | bytes 6176 | tf_op jit(solution)/shard_map/ppermute | solution.py:15
  210.2 0.1 pad_maximum_fusion
  210.3 4.0 %collective-permute-start.2 = (bf16[3,10,1]{2,1,0:T(8,128)(2,1)S(1)}, bf16[3,10,1]{2,1,0:T(8,128)(2,1)S(1)}, u32[]{:S(2)}, u32[]{:S(2)}) collective-permute-start(bf16[3,10,1]{2,1,0:T(8,128)(2,1)S(1)} %get-tuple-element.16), channel_id=1, source_target_pairs={{0,1},{1,2},{2,3},{3,4},{4,5},{5,6},{6,7},{8,9},{9,10},{10,11},{11... | collective-permute-start | bytes 188 | tf_op jit(solution)/shard_map/ppermute | solution.py:12
  214.3 1.3 collective-permute-start.3
  215.6 0.0 collective-permute-done.2
  215.7 3.7 %collective-permute-done.3 = bf16[3,10,1]{2,1,0:T(8,128)(2,1)S(1)} collective-permute-done((bf16[3,10,1]{2,1,0:T(8,128)(2,1)S(1)}, bf16[3,10,1]{2,1,0:T(8,128)(2,1)S(1)}, u32[]{:S(2)}, u32[]{:S(2)}) %collective-permute-start.3) | collective-permute-done | bytes 92 | tf_op jit(solution)/shard_map/ppermute | solution.py:15
  219.4 0.1 fusion.44
  219.5 0.7 add_convert_fusion
  (6 shorter events, 0.1 us)
Async XLA Ops:
  0.0 15.7 %copy-start = (bf16[1,3,528,256]{3,2,1,0:T(8,128)(2,1)S(1)}, bf16[1,3,528,256]{3,2,1,0:T(8,128)(2,1)}, u32[]{:S(2)}) copy-start(bf16[1,3,528,256]{3,2,1,0:T(8,128)(2,1)} %param.8) | copy-start | bytes 2433028
  1.7 20.8 %all-to-all-start = ((bf16[64,1,1]{2,1,0:T(2,128)(2,1)}), bf16[64,1,1]{2,1,0:T(2,128)(2,1)S(1)}, u32[]{:S(2)}, u32[]{:S(2)}) async-start(bf16[64,1,1]{2,1,0:T(2,128)(2,1)} %copy.27), calls=%async_computation | async-start | bytes 65536 | tf_op jit(solution)/shard_map/all_to_all | solution.py:62
  15.7 3.5 %copy-start.1 = (s32[1,33]{1,0:T(1,128)S(1)}, s32[1,33]{1,0:T(1,128)}, u32[]{:S(2)}) copy-start(s32[1,33]{1,0:T(1,128)} %param.11) | copy-start | bytes 400
  22.5 21.5 %all-to-all-start.2 = ((bf16[64,8,16]{2,1,0:T(8,128)(2,1)}), bf16[64,8,16]{2,1,0:T(8,128)(2,1)S(1)}, u32[]{:S(2)}, u32[]{:S(2)}) async-start(bf16[64,8,16]{2,1,0:T(8,128)(2,1)} %copy.30), calls=%async_computation.2 | async-start | bytes 262144 | tf_op jit(solution)/shard_map/all_to_all | solution.py:61
  44.0 151.3 %all-to-all-start.1 = ((bf16[64,3,16,1024]{3,2,1,0:T(8,128)(2,1)}), bf16[64,3,16,1024]{3,2,1,0:T(8,128)(2,1)}, u32[]{:S(2)}, u32[]{:S(2)}) async-start(bf16[64,3,16,1024]{3,2,1,0:T(8,128)(2,1)} %copy.29), calls=%async_computation.1 | async-start | bytes 12582912 | tf_op jit(solution)/shard_map/all_to_all | solution.py:60
  203.2 4.4 %collective-permute-start = (bf16[3,1,1024]{2,1,0:T(2,128)(2,1)S(1)}, bf16[3,1,1024]{2,1,0:T(2,128)(2,1)S(1)}, u32[]{:S(2)}, u32[]{:S(2)}) collective-permute-start(bf16[3,1,1024]{2,1,0:T(2,128)(2,1)S(1)} %get-tuple-element.17), channel_id=1, source_target_pairs={{0,8},{8,16},{16,24},{24,32},{32,40},{40,48},{48,56},{56,64},{64,7... | collective-permute-start | bytes 18440 | tf_op jit(solution)/shard_map/ppermute | solution.py:12
  205.2 5.0 %collective-permute-start.1 = (bf16[3,1,1024]{2,1,0:T(2,128)(2,1)S(1)}, bf16[3,1,1024]{2,1,0:T(2,128)(2,1)S(1)}, u32[]{:S(2)}, u32[]{:S(2)}) collective-permute-start(bf16[3,1,1024]{2,1,0:T(2,128)(2,1)S(1)} %get-tuple-element.18), channel_id=1, source_target_pairs={{8,0},{16,8},{24,16},{32,24},{40,32},{48,40},{56,48},{64,56},{72,6... | collective-permute-start | bytes 18440 | tf_op jit(solution)/shard_map/ppermute | solution.py:15
  210.3 5.4 %collective-permute-start.2 = (bf16[3,10,1]{2,1,0:T(8,128)(2,1)S(1)}, bf16[3,10,1]{2,1,0:T(8,128)(2,1)S(1)}, u32[]{:S(2)}, u32[]{:S(2)}) collective-permute-start(bf16[3,10,1]{2,1,0:T(8,128)(2,1)S(1)} %get-tuple-element.16), channel_id=1, source_target_pairs={{0,1},{1,2},{2,3},{3,4},{4,5},{5,6},{6,7},{8,9},{9,10},{10,11},{11... | collective-permute-start | bytes 188 | tf_op jit(solution)/shard_map/ppermute | solution.py:12
  214.3 5.1 %collective-permute-start.3 = (bf16[3,10,1]{2,1,0:T(8,128)(2,1)S(1)}, bf16[3,10,1]{2,1,0:T(8,128)(2,1)S(1)}, u32[]{:S(2)}, u32[]{:S(2)}) collective-permute-start(bf16[3,10,1]{2,1,0:T(8,128)(2,1)S(1)} %get-tuple-element.15), channel_id=1, source_target_pairs={{1,0},{2,1},{3,2},{4,3},{5,4},{6,5},{7,6},{9,8},{10,9},{11,10},{12... | collective-permute-start | bytes 188 | tf_op jit(solution)/shard_map/ppermute | solution.py:15
where the time goes:
time: 224 us; the launch traced here: 220 us
  waiting for transfers between devices  148 us (66%)
  starting transfers between devices  39.7 us (18%)
  matrix products  19.1 us (9%)
  local copies, waits for them, and re-layouts  9.37 us (4%)
  other arithmetic  3.59 us (2%)
    all_to_all x1, waiting for transfers between devices, body(): lax.all_to_all(out_segments, 'along', split_axis=0, concat_axis=0, tiled=...  139 us
    all_to_all x1, starting transfers between devices, body(): lax.all_to_all(slot_weight, 'along', split_axis=0, concat_axis=0, tiled=T...  11.6 us
    all_to_all x1, starting transfers between devices, body(): lax.all_to_all(out_segments, 'along', split_axis=0, concat_axis=0, tiled=...  10.5 us
    all_to_all x1, starting transfers between devices, body(): lax.all_to_all(out_rows, 'along', split_axis=0, concat_axis=0, tiled=True)  8.02 us
    dot_general x1, matrix products, body(): jnp.einsum('ns,csrt->ncrt', routing, col_part, preferred_element_type=jnp...  7.32 us
    ppermute x2, waiting for transfers between devices, with_halo(): lax.ppermute(lax.slice_in_dim(block, 0, width, axis=dim), axis, backward)  6.26 us
    convert_element_type x1, local copies, waits for them, and re-layouts, body(): out_segments = jnp.einsum('ns,csrt->ncrt', routing, col_part, preferred_e...  6.18 us
    ppermute x2, starting transfers between devices, with_halo(): lax.ppermute(lax.slice_in_dim(block, block.shape[dim] - width, None, axis...  5.91 us
  transfers between devices with their start and end apart: 7, of which 4 were waited for; matrix products, arithmetic and copies ran while one was open for 10% of the time, Pallas kernels for 0%

commit v1 on v0

v1 whole, which is shorter than its diff:
```python
import functools

import jax
import jax.numpy as jnp
from jax import lax
from jax.experimental import pallas as pl
from jax.experimental.pallas import tpu as pltpu
from jax.sharding import PartitionSpec as P

MESH = pl.DeviceIdType.MESH
F32 = jnp.float32
BF16 = jnp.bfloat16
NX, NY, NC = 4, 8, 2
PEERS = NX * NC
CHUNKS = ((4, 3), (5, 2), (6, 1), (7, 0))


def taps(delta, weights):
    value = jnp.zeros(delta.shape, F32)
    for step, weight in enumerate(weights):
        value = jnp.where(delta == float(step), weight, value)
    return value


def kernel(
    nz, frames, table, places, own_params, width_ref, out,
    image, lmat, outbox, inbox, params, cmat, ysend, yrecv, dsend, drecv, hsend, hrecv, ssend, srecv,
    load_sem, px_s, px_r, x_s, x_r, y_s, y_r, d_s, d_r, h_s, h_r,
):
    a = lax.axis_index("along")
    z = lax.axis_index("across")
    x, y, c = a // (NY * NC), (a // NC) % NY, a % NC

    def along(xx, yy, cc):
        return ((xx % NX) * NY + (yy % NY)) * NC + cc

    def x_peer(r):
        return (along(x + r % NX, y, (c + r // NX) % NC), z)

    def y_peer(rel):
        return (along(x, y + rel, c), z)

    after, before = (a + 1) % 64, (a + 63) % 64
    extra = (a + 63 + 2 * c) % 64
    barrier = pltpu.get_barrier_semaphore()
    friends = [x_peer(r) for r in range(1, PEERS)] + [y_peer(r) for r in range(1, NY)] + [(extra, z)]
    if nz > 1:
        friends += [(a, (z + 1) % nz), (a, (z + nz - 1) % nz)]
    for friend in friends:
        pl.semaphore_signal(barrier, inc=1, device_id=friend, device_id_type=MESH)

    load = pltpu.make_async_copy(frames.at[0], image.at[:, pl.ds(0, 528), :], load_sem)
    load.start()
    image[:, 528:, :] = jnp.zeros((3, 112, 256), BF16)

    row = lax.broadcasted_iota(jnp.int32, (128, 128), 0)
    lane = lax.broadcasted_iota(jnp.int32, (128, 128), 1)
    spread_row = lax.broadcasted_iota(jnp.int32, (128, 768), 0)
    spread_lane = lax.broadcasted_iota(jnp.int32, (128, 768), 1)
    spread = (spread_row // 8 == spread_lane // 128).astype(F32).astype(BF16)
    same = ((lane % 8) == (row % 8)).astype(F32)
    peer = row // 16
    group = (x + peer % NX) % NX
    core = (c + peer // NX) % NC
    first = (row // 8) % 2 == 0
    fp_row = places[0:1, :]
    start = places[0:1, 0:1]
    position = lax.broadcasted_iota(jnp.int32, (256, 128), 0).astype(F32)

    def make_matrix(r):
        def slab(n, carry):
            for half in range(2):
                j = n * 2 + half
                rows = [params[r, pl.ds(b * 8 + j, 1), :].astype(F32) for b in range(5)]
                value = taps(position - rows[4], rows[:4])
                cmat[n, r * 256:(r + 1) * 256, half * 128:(half + 1) * 128] = value.astype(BF16)
            return carry

        for n in range(4):
            slab(n, 0)

    def make_chunk(k):
        rel = jnp.where(first, CHUNKS[k][0], CHUNKS[k][1])
        tile = group * 16 + 2 * ((y + rel) % NY) + core
        hit = (tile == fp_row).astype(F32).astype(BF16)
        picked = jnp.dot(hit, table[...], preferred_element_type=F32) * same
        wide = jnp.dot(picked.astype(BF16), spread, preferred_element_type=F32)
        base = (lane - 16 * (tile - start)).astype(F32) - wide[:, :128]
        weights = [wide[:, 128 * (b + 1):128 * (b + 2)] for b in range(4)]
        for part in range(5):
            lmat[:, part * 128:(part + 1) * 128] = taps(base + float(128 * part), weights).astype(BF16)
        blend = jnp.concatenate([wide[:, 640:], wide[:, 640:]], axis=1)
        rows = [jnp.dot(lmat[...], image[ch], preferred_element_type=F32) * blend for ch in range(3)]
        for r in range(PEERS):
            block = jnp.concatenate(
                [rows[ch][r * 16 + m * 8:r * 16 + m * 8 + 8] for m in range(2) for ch in range(3)], axis=0
            ).astype(BF16)
            if r == 0:
                inbox[k, :, 0:256] = block
            else:
                outbox[k, r] = block

    def copy_params(r):
        return pltpu.make_async_remote_copy(
            src_ref=params.at[0], dst_ref=params.at[r], send_sem=px_s.at[r], recv_sem=px_r.at[r],
            device_id=x_peer(r), device_id_type=MESH,
        )

    def copy_chunk(k, r):
        return pltpu.make_async_remote_copy(
            src_ref=outbox.at[k, r], dst_ref=inbox.at[k, :, pl.ds(r * 256, 256)],
            send_sem=x_s.at[k, r], recv_sem=x_r.at[k, r], device_id=x_peer(r), device_id_type=MESH,
        )

    def copy_sum(rel):
        return pltpu.make_async_remote_copy(
            src_ref=ysend.at[rel], dst_ref=yrecv.at[rel], send_sem=y_s.at[rel], recv_sem=y_r.at[rel],
            device_id=y_peer(rel), device_id_type=MESH,
        )

    def copy_weight(rel):
        return pltpu.make_async_remote_copy(
            src_ref=dsend, dst_ref=drecv.at[rel], send_sem=d_s.at[rel], recv_sem=d_r.at[rel],
            device_id=y_peer(rel), device_id_type=MESH,
        )

    order = (2, 6, 1, 3, 5, 7, 4)
    params[0] = own_params[...]
    load.wait()
    make_chunk(0)
    pl.semaphore_wait(barrier, len(friends))
    for r in order:
        copy_params(r).start()
    for r in order:
        copy_chunk(0, r).start()
    for k in range(1, 4):
        make_chunk(k)
        for r in order:
            copy_chunk(k, r).start()
    make_matrix(0)
    weight = params[0, 32:48, :].astype(F32)
    for r in (4, 1, 3, 5, 7, 2, 6):
        copy_params(r).wait_recv()
        make_matrix(r)
        weight = weight + params[r, 32:48, :].astype(F32)
    weight = weight[8:16]
    dsend[...] = weight
    for rel in range(1, NY):
        copy_weight(rel).start()

    own = None
    for k in range(4):
        for r in range(1, PEERS):
            copy_chunk(k, r).wait_recv()
        left = inbox[k]
        total = jnp.concatenate(
            [jnp.dot(left, cmat[n], preferred_element_type=F32) for n in range(4)], axis=1
        )
        for m in range(2):
            rel = CHUNKS[k][m]
            part = total[m * 24:(m + 1) * 24]
            folded = jnp.concatenate([part[:, :512], part[:, 512:]], axis=0)
            if rel == 0:
                own = folded
            else:
                ysend[rel] = folded.astype(BF16)
                copy_sum(rel).start()

    for rel in range(1, NY):
        copy_weight(rel).wait_recv()
        weight = weight + drecv[rel]
    here = lax.broadcasted_iota(jnp.int32, (8, 128), 1) == a
    divisor = jnp.sum(jnp.where(here, weight, 0.0), axis=1, keepdims=True)[0:1]
    for rel in (4, 3, 5, 2, 6, 1, 7):
        copy_sum(rel).wait_recv()
        own = own + yrecv[rel].astype(F32)
    own = own / divisor
    values = jnp.concatenate([own[:24], own[24:]], axis=1).astype(BF16).astype(F32)

    blank = jnp.zeros((1, 256), F32)

    def edge_rows(i):
        pieces = []
        for j in range(4):
            pieces += [values[ch * 8 + i:ch * 8 + i + 1, j * 256:(j + 1) * 256] for ch in range(3)] + [blank]
        return jnp.concatenate(pieces, axis=0).astype(BF16)

    pad = jnp.zeros((8, 128), F32)
    hsend[0] = edge_rows(7)
    hsend[1] = edge_rows(0)
    ssend[0] = jnp.concatenate([values[:, 896:], pad], axis=0).astype(BF16)
    ssend[1] = jnp.concatenate([values[:, :128], pad], axis=0).astype(BF16)
    halo = [
        pltpu.make_async_remote_copy(
            src_ref=hsend.at[side], dst_ref=hrecv.at[side], send_sem=h_s.at[side], recv_sem=h_r.at[side],
            device_id=(after if side == 0 else before, z), device_id_type=MESH,
        )
        for side in range(2)
    ]
    if nz > 1:
        halo += [
            pltpu.make_async_remote_copy(
                src_ref=ssend.at[side], dst_ref=srecv.at[side], send_sem=h_s.at[2 + side],
                recv_sem=h_r.at[2 + side],
                device_id=(a, (z + 1) % nz if side == 0 else (z + nz - 1) % nz), device_id_type=MESH,
            )
            for side in range(2)
        ]
    for copy in halo:
        copy.start()
    for copy in halo:
        copy.wait_recv()

    def opened(side):
        got = hrecv[side].astype(F32)
        return [
            jnp.concatenate([got[4 * j + ch:4 * j + ch + 1] for j in range(4)], axis=1) for ch in range(3)
        ]

    width = width_ref[...].astype(F32)
    row8 = lax.broadcasted_iota(jnp.int32, (8, 1024), 0).astype(F32)
    col8 = lax.broadcasted_iota(jnp.int32, (8, 1024), 1).astype(F32)
    has_up = (a > 0).astype(F32)
    has_down = (a < 63).astype(F32)
    has_left = (z > 0).astype(F32)
    has_right = (z < nz - 1).astype(F32)
    top = 0.5 * jnp.maximum(0.0, 1.0 - row8 / width) * has_up
    bottom = 0.5 * jnp.maximum(0.0, 1.0 - (7.0 - row8) / width) * has_down
    ramp_left = 0.5 * jnp.maximum(0.0, 1.0 - col8 / width) * has_left
    ramp_right = 0.5 * jnp.maximum(0.0, 1.0 - (1023.0 - col8) / width) * has_right
    up, down = opened(0), opened(1)
    for ch in range(3):
        tile = values[ch * 8:(ch + 1) * 8]
        result = tile + top * (up[ch] - tile[0:1]) + bottom * (down[ch] - tile[7:8])
        if nz > 1:
            left_col = srecv[0, ch * 8:(ch + 1) * 8, 127:128].astype(F32)
            right_col = srecv[1, ch * 8:(ch + 1) * 8, 0:1].astype(F32)
            result = result + ramp_left * (left_col - tile[:, 0:1]) + ramp_right * (right_col - tile[:, 1023:])
        out[ch] = result.astype(BF16)

    for r in range(1, PEERS):
        copy_params(r).wait_send()
        for k in range(4):
            copy_chunk(k, r).wait_send()
    for rel in range(1, NY):
        copy_weight(rel).wait_send()
        copy_sum(rel).wait_send()
    for copy in halo:
        copy.wait_send()


def body(
    frames, col_start, col_weights, footprint, row_start, row_weights, seg_weight, feather_width
):
    nz = lax.axis_size("across")
    blend = jnp.broadcast_to(seg_weight[0][:, None], (33, 8))
    table = jnp.concatenate(
        [row_start[0].astype(BF16), row_weights[0].reshape(33, 32), blend], axis=1
    )
    table = jnp.pad(table, ((0, 95), (0, 80)))
    places = jnp.broadcast_to(jnp.pad(footprint, ((0, 0), (0, 95)), constant_values=-1), (8, 128))
    tiles = jnp.arange(128, dtype=jnp.int32)
    by_tile = jnp.sum(
        jnp.where(footprint[0][:, None] == tiles[None, :], seg_weight[0].astype(F32)[:, None], 0.0), axis=0
    ).astype(BF16)
    own_params = jnp.concatenate(
        [
            col_weights[0].reshape(32, 128),
            col_start[0].astype(BF16).reshape(8, 128),
            jnp.broadcast_to(by_tile[None, :], (8, 128)),
        ],
        axis=0,
    )
    vmem = pl.BlockSpec(memory_space=pltpu.VMEM)
    dma = pltpu.SemaphoreType.DMA
    return pl.pallas_call(
        functools.partial(kernel, nz),
        out_shape=jax.ShapeDtypeStruct((3, 8, 1024), BF16),
        in_specs=[pl.BlockSpec(memory_space=pl.ANY), vmem, vmem, vmem, vmem],
        out_specs=vmem,
        scratch_shapes=[
            pltpu.VMEM((3, 640, 256), BF16),
            pltpu.VMEM((128, 640), BF16),
            pltpu.VMEM((4, PEERS, 48, 256), BF16),
            pltpu.VMEM((4, 48, 256 * PEERS), BF16),
            pltpu.VMEM((PEERS, 48, 128), BF16),
            pltpu.VMEM((4, 256 * PEERS, 256), BF16),
            pltpu.VMEM((NY, 48, 512), BF16),
            pltpu.VMEM((NY, 48, 512), BF16),
            pltpu.VMEM((8, 128), F32),
            pltpu.VMEM((NY, 8, 128), F32),
            pltpu.VMEM((2, 16, 256), BF16),
            pltpu.VMEM((2, 16, 256), BF16),
            pltpu.VMEM((2, 32, 128), BF16),
            pltpu.VMEM((2, 32, 128), BF16),
            dma,
            dma((PEERS,)),
            dma((PEERS,)),
            dma((4, PEERS)),
            dma((4, PEERS)),
            dma((NY,)),
            dma((NY,)),
            dma((NY,)),
            dma((NY,)),
            dma((4,)),
            dma((4,)),
        ],
        compiler_params=pltpu.CompilerParams(
            collective_id=0, has_side_effects=True, vmem_limit_bytes=32 * 2**20
        ),
    )(frames, table, places, own_params, feather_width)


def solution(mesh):
    placed = (
        P("along", None, None, "across"),
        P("along", "across"),
        P("along", None, "across"),
        P("along", None),
        P("along", None, None),
        P("along", None, None, None),
        P("along", None),
        P("along", "across"),
    )
    return jax.shard_map(
        body, mesh=mesh, in_specs=placed, out_specs=P(None, "along", "across"), check_vma=False
    )
```

time: 224 us -> 43.4 us (0.19); the launches traced: 220 us -> 43.1 us
  waiting for transfers between devices: 148 us -> 0 us
  starting transfers between devices: 39.7 us -> 0 us
  Pallas kernels: 0 us -> 37.6 us
  matrix products: 19.1 us -> 0 us
  local copies, waits for them, and re-layouts: 9.37 us -> 4.55 us
  other arithmetic: 3.59 us -> 0.22 us
    all_to_all x3 -> x0, waiting for transfers between devices: 141 us -> none  [the longest x1 139 us: body(): lax.all_to_all(out_segments, 'along', split_axis=0, concat_axis=0, tiled=...]
    pallas_call x0 -> x1, Pallas kernels: none -> 37.6 us  [body(): pl.pallas_call(functools.partial(kernel, nz), out_shape=jax.ShapeDtypeStr...]
    all_to_all x3 -> x0, starting transfers between devices: 30.1 us -> none  [the longest x1 11.6 us: body(): lax.all_to_all(slot_weight, 'along', split_axis=0, concat_axis=0, tiled=T...]
    dot_general x5 -> x0, matrix products: 18.9 us -> none  [the longest x1 7.32 us: body(): jnp.einsum('ns,csrt->ncrt', routing, col_part, preferred_element_type=jnp...]
    ppermute x4 -> x0, starting transfers between devices: 9.61 us -> none  [the longest x2 5.91 us: with_halo(): lax.ppermute(lax.slice_in_dim(block, block.shape[dim] - width, None, axis...]
    convert_element_type x2 -> x0, local copies, waits for them, and re-layouts: 6.95 us -> none  [the longest x1 6.18 us: body(): out_segments = jnp.einsum('ns,csrt->ncrt', routing, col_part, preferred_e...]
    ppermute x4 -> x0, waiting for transfers between devices: 6.27 us -> none  [the longest x2 6.26 us: with_halo(): lax.ppermute(lax.slice_in_dim(block, 0, width, axis=dim), axis, backward)]
    unnamed x5 -> x16, local copies, waits for them, and re-layouts: 0.02 us -> 4.35 us
  transfers between devices with their start and end apart: 7 -> 0, of which waited for: 4 -> 0; matrix products, arithmetic and copies ran while one was open for 10% -> 0% of each run, Pallas kernels for 0% -> 0%
where the time goes in v1:
time: 43.4 us; the launch traced here: 43.1 us
  Pallas kernels  37.6 us (87%)
  local copies, waits for them, and re-layouts  4.55 us (10%)
  between operations  0.73 us (2%)
    pallas_call x1, Pallas kernels, body(): pl.pallas_call(functools.partial(kernel, nz), out_shape=jax.ShapeDtypeStr...  37.6 us
    unnamed x16, local copies, waits for them, and re-layouts  4.35 us

profile of v1, /device:TPU:1, one launch (start us, length us, event | category | flops | bytes accessed | tf_op | source)
XLA Modules:
  0.0 43.1 jit_solution(12626318608893727183)
XLA Ops:
  0.7 0.0 copy-start.6
  0.7 0.0 copy-start.5
  0.7 0.6 %copy-done.6 = s32[1,33]{1,0:T(1,128)S(1)} copy-done((s32[1,33]{1,0:T(1,128)S(1)}, s32[1,33]{1,0:T(1,128)}, u32[]{:S(2)}) %copy-start.6) | copy-done | bytes 156
  1.3 0.0 copy-start.3
  1.3 0.0 copy-done.5
  1.3 0.0 copy-start.1
  1.3 0.1 select_reduce_fusion
  1.4 0.5 %copy-done.3 = s32[1,1024]{1,0:T(1,128)S(1)} copy-done((s32[1,1024]{1,0:T(1,128)S(1)}, s32[1,1024]{1,0:T(1,128)}, u32[]{:S(2)}) %copy-start.3) | copy-done | bytes 4120
  2.0 0.0 copy-done.1
  2.1 0.0 copy-start.2
  2.1 0.7 %copy-done.2 = bf16[1,33,4,8]{1,3,2,0:T(8,128)(2,1)S(1)} copy-done((bf16[1,33,4,8]{1,3,2,0:T(8,128)(2,1)S(1)}, bf16[1,33,4,8]{1,3,2,0:T(8,128)(2,1)}, u32[]{:S(2)}) %copy-start.2) | copy-done | bytes 2136
  2.8 0.1 copy.14
  2.9 0.0 copy-start.4
  2.9 0.1 broadcast_in_dim.35
  2.9 0.6 %copy-done.4 = s32[1,33,8]{1,2,0:T(8,128)S(1)} copy-done((s32[1,33,8]{1,2,0:T(8,128)S(1)}, s32[1,33,8]{1,2,0:T(8,128)}, u32[]{:S(2)}) %copy-start.4) | copy-done | bytes 1080
  3.5 0.1 copy.13
  3.6 0.1 fusion.8.table
  3.7 0.0 copy-start
  3.7 1.1 %copy-done = bf16[1,3,528,256]{3,2,1,0:T(8,128)(2,1)S(1)} copy-done((bf16[1,3,528,256]{3,2,1,0:T(8,128)(2,1)S(1)}, bf16[1,3,528,256]{3,2,1,0:T(8,128)(2,1)}, u32[]{:S(2)}) %copy-start) | copy-done | bytes 811032
  4.9 37.6 %shard_map.82 = bf16[3,8,1024]{2,1,0:T(8,128)(2,1)S(1)} custom-call(bf16[1,3,528,256]{3,2,1,0:T(8,128)(2,1)S(1)} %copy-done, bf16[128,128]{1,0:T(8,128)(2,1)S(1)} %fusion.8.table, s32[8,128]{1,0:T(8,128)S(1)} %broadcast_in_dim.37.places, bf16[48,128]{1,0:T(8,128)(2,1)S(1)} %pad_maximum_fusion.own_params, s32[1,1]{1,0:T(1,128)S(6)} %copy.16.width_ref), custom_call_target="tpu_custom_call" | custom-call | tf_op jit(solution)/shard_map/pallas_call | solution.py:276
  42.5 0.6 %copy.17 = bf16[3,8,1024]{2,1,0:T(8,128)(2,1)} copy(bf16[3,8,1024]{2,1,0:T(8,128)(2,1)S(1)} %shard_map.82) | data formatting | bytes 98304
  (8 shorter events, 0.1 us)
Async XLA Ops:
  0.7 0.7 %copy-start.6 = (s32[1,33]{1,0:T(1,128)S(1)}, s32[1,33]{1,0:T(1,128)}, u32[]{:S(2)}) copy-start(s32[1,33]{1,0:T(1,128)} %param.11) | copy-start | bytes 400
  0.7 0.7 %copy-start.5 = (bf16[1,33]{1,0:T(2,128)(2,1)S(1)}, bf16[1,33]{1,0:T(2,128)(2,1)}, u32[]{:S(2)}) copy-start(bf16[1,33]{1,0:T(2,128)(2,1)} %param.14) | copy-start | bytes 202
  1.3 0.7 %copy-start.3 = (s32[1,1024]{1,0:T(1,128)S(1)}, s32[1,1024]{1,0:T(1,128)}, u32[]{:S(2)}) copy-start(s32[1,1024]{1,0:T(1,128)} %param.9) | copy-start | bytes 12292
  1.3 0.7 %copy-start.1 = (bf16[1,4,1024]{2,1,0:T(4,128)(2,1)S(1)}, bf16[1,4,1024]{2,1,0:T(4,128)(2,1)}, u32[]{:S(2)}) copy-start(bf16[1,4,1024]{2,1,0:T(4,128)(2,1)} %param.10) | copy-start | bytes 24580
  2.1 0.7 %copy-start.2 = (bf16[1,33,4,8]{1,3,2,0:T(8,128)(2,1)S(1)}, bf16[1,33,4,8]{1,3,2,0:T(8,128)(2,1)}, u32[]{:S(2)}) copy-start(bf16[1,33,4,8]{1,3,2,0:T(8,128)(2,1)} %param.13) | copy-start | bytes 6340
  2.9 0.7 %copy-start.4 = (s32[1,33,8]{1,2,0:T(8,128)S(1)}, s32[1,33,8]{1,2,0:T(8,128)}, u32[]{:S(2)}) copy-start(s32[1,33,8]{1,2,0:T(8,128)} %param.12) | copy-start | bytes 3172
  3.7 1.1 %copy-start = (bf16[1,3,528,256]{3,2,1,0:T(8,128)(2,1)S(1)}, bf16[1,3,528,256]{3,2,1,0:T(8,128)(2,1)}, u32[]{:S(2)}) copy-start(bf16[1,3,528,256]{3,2,1,0:T(8,128)(2,1)} %frames.1) | copy-start | bytes 2433028

commit v2 on v1

--- a/solution.py
+++ b/solution.py
@@ -13,19 +13,22 @@
 NX, NY, NC = 4, 8, 2
 PEERS = NX * NC
 CHUNKS = ((4, 3), (5, 2), (6, 1), (7, 0))
+GROUPS = ((0, 4), (1, 5), (3, 7), (2, 6))
+PLACE = {r: 2 * g + i for g, group in enumerate(GROUPS) for i, r in enumerate(group)}
 
 
 def taps(delta, weights):
-    value = jnp.zeros(delta.shape, F32)
+    value = jnp.zeros(delta.shape, delta.dtype)
     for step, weight in enumerate(weights):
-        value = jnp.where(delta == float(step), weight, value)
+        value = jnp.where(delta == jnp.asarray(step, delta.dtype), weight, value)
     return value
 
 
 def kernel(
-    nz, frames, table, places, own_params, width_ref, out,
-    image, lmat, outbox, inbox, params, cmat, ysend, yrecv, dsend, drecv, hsend, hrecv, ssend, srecv,
-    load_sem, px_s, px_r, x_s, x_r, y_s, y_r, d_s, d_r, h_s, h_r,
+    nz, frames, col_start, col_weights, footprint, row_start, row_weights, seg_weight, feather, out,
+    image, starts_in, taps_in, places_in, rstart_in, rtaps_in, blend_in, width_in,
+    table, places, blends, gather, lmat, outbox, inbox, params, cmat, ysend, yrecv, dsend, drecv, hsend, hrecv, ssend, srecv,
+    load_sem, small_sem, px_s, px_r, x_s, x_r, y_s, y_r, d_s, d_r, h_s, h_r,
 ):
     a = lax.axis_index("along")
     z = lax.axis_index("across")
@@ -51,12 +54,38 @@
 
     load = pltpu.make_async_copy(frames.at[0], image.at[:, pl.ds(0, 528), :], load_sem)
     load.start()
+    small = [
+        pltpu.make_async_copy(src, dst, small_sem.at[i])
+        for i, (src, dst) in enumerate(
+            (
+                (footprint, places_in),
+                (row_start.at[0], rstart_in),
+                (row_weights.at[0], rtaps_in),
+                (seg_weight, blend_in),
+                (col_weights.at[0], taps_in),
+                (col_start, starts_in),
+                (feather, width_in),
+            )
+        )
+    ]
+    for copy in small:
+        copy.start()
     image[:, 528:, :] = jnp.zeros((3, 112, 256), BF16)
+    places[...] = jnp.full((8, 128), -1, jnp.int32)
+    blends[...] = jnp.zeros((8, 128), F32)
+    for copy in small:
+        copy.wait()
+    places[0:1, 0:33] = places_in[...]
+    blends[0:1, 0:33] = blend_in[...].astype(F32)
+    table[...] = jnp.zeros((128, 128), F32)
+    table[0:8, 0:33] = rstart_in[...].astype(F32)
+    for b in range(4):
+        table[8 * (b + 1):8 * (b + 2), 0:33] = rtaps_in[b].astype(F32)
 
     row = lax.broadcasted_iota(jnp.int32, (128, 128), 0)
     lane = lax.broadcasted_iota(jnp.int32, (128, 128), 1)
-    spread_row = lax.broadcasted_iota(jnp.int32, (128, 768), 0)
-    spread_lane = lax.broadcasted_iota(jnp.int32, (128, 768), 1)
+    spread_row = lax.broadcasted_iota(jnp.int32, (128, 640), 0)
+    spread_lane = lax.broadcasted_iota(jnp.int32, (128, 640), 1)
     spread = (spread_row // 8 == spread_lane // 128).astype(F32).astype(BF16)
     same = ((lane % 8) == (row % 8)).astype(F32)
     peer = row // 16
@@ -65,31 +94,41 @@
     first = (row // 8) % 2 == 0
     fp_row = places[0:1, :]
     start = places[0:1, 0:1]
-    position = lax.broadcasted_iota(jnp.int32, (256, 128), 0).astype(F32)
+    blend_row = blends[0:1, :]
+    ones = jnp.ones((128, 128), BF16)
+    rows_table = table[...].astype(BF16)
+    by_tile = jnp.dot(
+        blends[...].astype(BF16), (lane - start == row).astype(F32).astype(BF16), preferred_element_type=F32
+    )
+    col_taps = taps_in[...].astype(F32)
+    col_first = starts_in[...].astype(F32)
+    for j in range(8):
+        for b in range(4):
+            gather[b * 8 + j:b * 8 + j + 1, :] = col_taps[b:b + 1, j * 128:(j + 1) * 128]
+        gather[32 + j:33 + j, :] = col_first[:, j * 128:(j + 1) * 128]
+    gather[40:48, :] = by_tile
+    position = lax.broadcasted_iota(jnp.int32, (256, 128), 0).astype(F32).astype(BF16)
 
     def make_matrix(r):
-        def slab(n, carry):
-            for half in range(2):
-                j = n * 2 + half
-                rows = [params[r, pl.ds(b * 8 + j, 1), :].astype(F32) for b in range(5)]
-                value = taps(position - rows[4], rows[:4])
-                cmat[n, r * 256:(r + 1) * 256, half * 128:(half + 1) * 128] = value.astype(BF16)
-            return carry
-
-        for n in range(4):
-            slab(n, 0)
+        for j in range(8):
+            rows = [params[r, b * 8 + j:b * 8 + j + 1, :] for b in range(5)]
+            value = taps(position - rows[4], rows[:4])
+            cmat[j // 2, PLACE[r] * 256:(PLACE[r] + 1) * 256, (j % 2) * 128:(j % 2 + 1) * 128] = value
 
     def make_chunk(k):
         rel = jnp.where(first, CHUNKS[k][0], CHUNKS[k][1])
         tile = group * 16 + 2 * ((y + rel) % NY) + core
-        hit = (tile == fp_row).astype(F32).astype(BF16)
-        picked = jnp.dot(hit, table[...], preferred_element_type=F32) * same
+        hit = (tile == fp_row).astype(F32)
+        picked = same * lax.dot_general(
+            hit.astype(BF16), rows_table, (((1,), (1,)), ((), ())), preferred_element_type=F32
+        )
+        blend = jnp.dot((hit * blend_row).astype(BF16), ones, preferred_element_type=F32)
         wide = jnp.dot(picked.astype(BF16), spread, preferred_element_type=F32)
         base = (lane - 16 * (tile - start)).astype(F32) - wide[:, :128]
         weights = [wide[:, 128 * (b + 1):128 * (b + 2)] for b in range(4)]
         for part in range(5):
             lmat[:, part * 128:(part + 1) * 128] = taps(base + float(128 * part), weights).astype(BF16)
-        blend = jnp.concatenate([wide[:, 640:], wide[:, 640:]], axis=1)
+        blend = jnp.concatenate([blend, blend], axis=1)
         rows = [jnp.dot(lmat[...], image[ch], preferred_element_type=F32) * blend for ch in range(3)]
         for r in range(PEERS):
             block = jnp.concatenate(
@@ -102,20 +141,22 @@
 
     def copy_params(r):
         return pltpu.make_async_remote_copy(
-            src_ref=params.at[0], dst_ref=params.at[r], send_sem=px_s.at[r], recv_sem=px_r.at[r],
-            device_id=x_peer(r), device_id_type=MESH,
+            src_ref=params.at[max(r - NX, 0)], dst_ref=params.at[r], send_sem=px_s.at[r], recv_sem=px_r.at[r],
+            device_id=x_peer(min(r, NX)), device_id_type=MESH,
         )
 
     def copy_chunk(k, r):
         return pltpu.make_async_remote_copy(
-            src_ref=outbox.at[k, r], dst_ref=inbox.at[k, :, pl.ds(r * 256, 256)],
+            src_ref=outbox.at[k, r], dst_ref=inbox.at[k, :, pl.ds(PLACE[r] * 256, 256)],
             send_sem=x_s.at[k, r], recv_sem=x_r.at[k, r], device_id=x_peer(r), device_id_type=MESH,
         )
 
-    def copy_sum(rel):
+    def copy_sum(slot):
+        hop = {0: 6, 1: 1, 2: 2, 3: 1, 4: 2, 5: 7, 6: 6, 7: 7}[slot]
+        lanes = {0: pl.ds(256, 256), 4: pl.ds(0, 256)}.get(slot, pl.ds(0, 512))
         return pltpu.make_async_remote_copy(
-            src_ref=ysend.at[rel], dst_ref=yrecv.at[rel], send_sem=y_s.at[rel], recv_sem=y_r.at[rel],
-            device_id=y_peer(rel), device_id_type=MESH,
+            src_ref=ysend.at[slot or 4, :, lanes], dst_ref=yrecv.at[slot, :, lanes],
+            send_sem=y_s.at[slot], recv_sem=y_r.at[slot], device_id=y_peer(hop), device_id_type=MESH,
         )
 
     def copy_weight(rel):
@@ -125,22 +166,29 @@
         )
 
     order = (2, 6, 1, 3, 5, 7, 4)
-    params[0] = own_params[...]
+    params[0] = gather[...].astype(BF16)
     load.wait()
     make_chunk(0)
     pl.semaphore_wait(barrier, len(friends))
-    for r in order:
+    for r in (2, 1, 3, 4):
         copy_params(r).start()
     for r in order:
         copy_chunk(0, r).start()
-    for k in range(1, 4):
-        make_chunk(k)
-        for r in order:
-            copy_chunk(k, r).start()
+    make_chunk(1)
+    for r in order:
+        copy_chunk(1, r).start()
+    make_chunk(2)
+    for r in order:
+        copy_chunk(2, r).start()
+    make_chunk(3)
+    for r in order:
+        copy_chunk(3, r).start()
     make_matrix(0)
     weight = params[0, 32:48, :].astype(F32)
-    for r in (4, 1, 3, 5, 7, 2, 6):
+    for r in (4, 1, 3, 2, 5, 7, 6):
         copy_params(r).wait_recv()
+        if r < NX:
+            copy_params(r + NX).start()
         make_matrix(r)
         weight = weight + params[r, 32:48, :].astype(F32)
     weight = weight[8:16]
@@ -148,30 +196,45 @@
     for rel in range(1, NY):
         copy_weight(rel).start()
 
-    own = None
+    held = {}
     for k in range(4):
-        for r in range(1, PEERS):
-            copy_chunk(k, r).wait_recv()
-        left = inbox[k]
-        total = jnp.concatenate(
-            [jnp.dot(left, cmat[n], preferred_element_type=F32) for n in range(4)], axis=1
-        )
+        total = [0.0] * 4
+        for g, group in enumerate(GROUPS):
+            for r in group:
+                if r:
+                    copy_chunk(k, r).wait_recv()
+            left = inbox[k, :, g * 512:(g + 1) * 512]
+            total = [
+                total[n] + jnp.dot(left, cmat[n, g * 512:(g + 1) * 512], preferred_element_type=F32)
+                for n in range(4)
+            ]
+        total = jnp.concatenate(total, axis=1)
         for m in range(2):
             rel = CHUNKS[k][m]
             part = total[m * 24:(m + 1) * 24]
-            folded = jnp.concatenate([part[:, :512], part[:, 512:]], axis=0)
-            if rel == 0:
-                own = folded
-            else:
+            held[rel] = folded = jnp.concatenate([part[:, :512], part[:, 512:]], axis=0)
+            if rel in (1, 3, 4, 5, 7):
                 ysend[rel] = folded.astype(BF16)
                 copy_sum(rel).start()
+            if rel == 4:
+                copy_sum(0).start()
+        if k == 2:
+            for rel, near, far, lanes in ((2, 3, 4, 0), (6, 5, 0, 256)):
+                copy_sum(near).wait_recv()
+                copy_sum(far).wait_recv()
+                half = yrecv[far, :, lanes:lanes + 256].astype(F32)
+                blank = jnp.zeros((48, 256), F32)
+                half = jnp.concatenate([blank, half] if lanes else [half, blank], axis=1)
+                ysend[rel] = (held[rel] + yrecv[near].astype(F32) + half).astype(BF16)
+                copy_sum(rel).start()
+    own = held[0]
 
     for rel in range(1, NY):
         copy_weight(rel).wait_recv()
         weight = weight + drecv[rel]
     here = lax.broadcasted_iota(jnp.int32, (8, 128), 1) == a
     divisor = jnp.sum(jnp.where(here, weight, 0.0), axis=1, keepdims=True)[0:1]
-    for rel in (4, 3, 5, 2, 6, 1, 7):
+    for rel in (2, 6, 1, 7):
         copy_sum(rel).wait_recv()
         own = own + yrecv[rel].astype(F32)
     own = own / divisor
@@ -217,7 +280,7 @@
             jnp.concatenate([got[4 * j + ch:4 * j + ch + 1] for j in range(4)], axis=1) for ch in range(3)
         ]
 
-    width = width_ref[...].astype(F32)
+    width = width_in[...].astype(F32)
     row8 = lax.broadcasted_iota(jnp.int32, (8, 1024), 0).astype(F32)
     col8 = lax.broadcasted_iota(jnp.int32, (8, 1024), 1).astype(F32)
     has_up = (a > 0).astype(F32)
@@ -244,7 +307,8 @@
             copy_chunk(k, r).wait_send()
     for rel in range(1, NY):
         copy_weight(rel).wait_send()
-        copy_sum(rel).wait_send()
+    for slot in range(NY):
+        copy_sum(slot).wait_send()
     for copy in halo:
         copy.wait_send()
 
@@ -253,33 +317,26 @@
     frames, col_start, col_weights, footprint, row_start, row_weights, seg_weight, feather_width
 ):
     nz = lax.axis_size("across")
-    blend = jnp.broadcast_to(seg_weight[0][:, None], (33, 8))
-    table = jnp.concatenate(
-        [row_start[0].astype(BF16), row_weights[0].reshape(33, 32), blend], axis=1
-    )
-    table = jnp.pad(table, ((0, 95), (0, 80)))
-    places = jnp.broadcast_to(jnp.pad(footprint, ((0, 0), (0, 95)), constant_values=-1), (8, 128))
-    tiles = jnp.arange(128, dtype=jnp.int32)
-    by_tile = jnp.sum(
-        jnp.where(footprint[0][:, None] == tiles[None, :], seg_weight[0].astype(F32)[:, None], 0.0), axis=0
-    ).astype(BF16)
-    own_params = jnp.concatenate(
-        [
-            col_weights[0].reshape(32, 128),
-            col_start[0].astype(BF16).reshape(8, 128),
-            jnp.broadcast_to(by_tile[None, :], (8, 128)),
-        ],
-        axis=0,
-    )
     vmem = pl.BlockSpec(memory_space=pltpu.VMEM)
     dma = pltpu.SemaphoreType.DMA
     return pl.pallas_call(
         functools.partial(kernel, nz),
         out_shape=jax.ShapeDtypeStruct((3, 8, 1024), BF16),
-        in_specs=[pl.BlockSpec(memory_space=pl.ANY), vmem, vmem, vmem, vmem],
+        in_specs=[pl.BlockSpec(memory_space=pltpu.HBM)] * 8,
         out_specs=vmem,
         scratch_shapes=[
             pltpu.VMEM((3, 640, 256), BF16),
+            pltpu.VMEM((1, 1024), jnp.int32),
+            pltpu.VMEM((4, 1024), BF16),
+            pltpu.VMEM((1, 33), jnp.int32),
+            pltpu.VMEM((8, 33), jnp.int32),
+            pltpu.VMEM((4, 8, 33), BF16),
+            pltpu.VMEM((1, 33), BF16),
+            pltpu.VMEM((1, 1), jnp.int32),
+            pltpu.VMEM((128, 128), F32),
+            pltpu.VMEM((8, 128), jnp.int32),
+            pltpu.VMEM((8, 128), F32),
+            pltpu.VMEM((48, 128), F32),
             pltpu.VMEM((128, 640), BF16),
             pltpu.VMEM((4, PEERS, 48, 256), BF16),
             pltpu.VMEM((4, 48, 256 * PEERS), BF16),
@@ -294,6 +351,7 @@
             pltpu.VMEM((2, 32, 128), BF16),
             pltpu.VMEM((2, 32, 128), BF16),
             dma,
+            dma((7,)),
             dma((PEERS,)),
             dma((PEERS,)),
             dma((4, PEERS)),
@@ -306,9 +364,12 @@
             dma((4,)),
         ],
         compiler_params=pltpu.CompilerParams(
-            collective_id=0, has_side_effects=True, vmem_limit_bytes=32 * 2**20
+            collective_id=0, has_side_effects=True, vmem_limit_bytes=60 * 2**20
         ),
-    )(frames, table, places, own_params, feather_width)
+    )(
+        frames, col_start, col_weights, footprint, jnp.transpose(row_start, (0, 2, 1)),
+        jnp.transpose(row_weights, (0, 2, 3, 1)), seg_weight, feather_width,
+    )
 
 
 def solution(mesh):

time: 43.4 us -> 38.9 us (0.90)
  local copies, waits for them, and re-layouts: 4.55 us -> 1.42 us
  Pallas kernels: 37.6 us -> 36.6 us
    unnamed x16 -> x1, local copies, waits for them, and re-layouts: 4.35 us -> 1.42 us
    pallas_call x1, Pallas kernels: 37.6 us -> 36.6 us  [body(): pl.pallas_call(functools.partial(kernel, nz), out_shape=jax.ShapeDtypeStr...]
where the time goes in v2:
time: 38.9 us; the launch traced here: 38.7 us
  Pallas kernels  36.6 us (94%)
  local copies, waits for them, and re-layouts  1.42 us (4%)
  between operations  0.66 us (2%)
    pallas_call x1, Pallas kernels, body(): pl.pallas_call(functools.partial(kernel, nz), out_shape=jax.ShapeDtypeStr...  36.6 us
    unnamed x1, local copies, waits for them, and re-layouts  1.42 us

profile of v2, /device:TPU:1, one launch (start us, length us, event | category | flops | bytes accessed | tf_op | source)
XLA Modules:
  0.0 38.7 jit_solution(680883163357519301)
XLA Ops:
  0.7 36.6 %shard_map.82 = bf16[3,8,1024]{2,1,0:T(8,128)(2,1)} custom-call(bf16[1,3,528,256]{3,2,1,0:T(8,128)(2,1)} %frames.1, s32[1,1024]{1,0:T(1,128)} %col_start.1, bf16[1,4,1024]{2,1,0:T(4,128)(2,1)} %col_weights.1, s32[1,33]{1,0:T(1,128)} %footprint.1, s32[1,8,33]{2,1,0:T(8,128)} %bitcast.3, bf16[1,4,8,33]{3,2,1,0:T(8,128)(2,1)} %bitcast.2, ...), custom_call_target="tpu_custom_call" | custom-call | tf_op jit(solution)/shard_map/pallas_call | solution.py:322
  37.3 1.4 %copy.11 = bf16[3,8,1024]{2,1,0:T(8,128)(2,1)} copy(bf16[3,8,1024]{2,1,0:T(8,128)(2,1)} %shard_map.82) | data formatting | bytes 98304

commit v3 on v2

--- a/solution.py
+++ b/solution.py
@@ -12,7 +12,7 @@
 BF16 = jnp.bfloat16
 NX, NY, NC = 4, 8, 2
 PEERS = NX * NC
-CHUNKS = ((4, 3), (5, 2), (6, 1), (7, 0))
+CHUNKS = ((5, 3), (4, 2), (6, 1), (7, 0))
 GROUPS = ((0, 4), (1, 5), (3, 7), (2, 6))
 PLACE = {r: 2 * g + i for g, group in enumerate(GROUPS) for i, r in enumerate(group)}
 
@@ -152,10 +152,9 @@
         )
 
     def copy_sum(slot):
-        hop = {0: 6, 1: 1, 2: 2, 3: 1, 4: 2, 5: 7, 6: 6, 7: 7}[slot]
-        lanes = {0: pl.ds(256, 256), 4: pl.ds(0, 256)}.get(slot, pl.ds(0, 512))
+        hop = {1: 1, 2: 2, 3: 1, 4: 4, 5: 7, 6: 6, 7: 7}[slot]
         return pltpu.make_async_remote_copy(
-            src_ref=ysend.at[slot or 4, :, lanes], dst_ref=yrecv.at[slot, :, lanes],
+            src_ref=ysend.at[slot], dst_ref=yrecv.at[slot],
             send_sem=y_s.at[slot], recv_sem=y_r.at[slot], device_id=y_peer(hop), device_id_type=MESH,
         )
 
@@ -216,16 +215,10 @@
             if rel in (1, 3, 4, 5, 7):
                 ysend[rel] = folded.astype(BF16)
                 copy_sum(rel).start()
-            if rel == 4:
-                copy_sum(0).start()
         if k == 2:
-            for rel, near, far, lanes in ((2, 3, 4, 0), (6, 5, 0, 256)):
+            for rel, near in ((2, 3), (6, 5)):
                 copy_sum(near).wait_recv()
-                copy_sum(far).wait_recv()
-                half = yrecv[far, :, lanes:lanes + 256].astype(F32)
-                blank = jnp.zeros((48, 256), F32)
-                half = jnp.concatenate([blank, half] if lanes else [half, blank], axis=1)
-                ysend[rel] = (held[rel] + yrecv[near].astype(F32) + half).astype(BF16)
+                ysend[rel] = (held[rel] + yrecv[near].astype(F32)).astype(BF16)
                 copy_sum(rel).start()
     own = held[0]
 
@@ -234,7 +227,7 @@
         weight = weight + drecv[rel]
     here = lax.broadcasted_iota(jnp.int32, (8, 128), 1) == a
     divisor = jnp.sum(jnp.where(here, weight, 0.0), axis=1, keepdims=True)[0:1]
-    for rel in (2, 6, 1, 7):
+    for rel in (4, 2, 6, 1, 7):
         copy_sum(rel).wait_recv()
         own = own + yrecv[rel].astype(F32)
     own = own / divisor
@@ -271,8 +264,6 @@
         ]
     for copy in halo:
         copy.start()
-    for copy in halo:
-        copy.wait_recv()
 
     def opened(side):
         got = hrecv[side].astype(F32)
@@ -291,14 +282,22 @@
     bottom = 0.5 * jnp.maximum(0.0, 1.0 - (7.0 - row8) / width) * has_down
     ramp_left = 0.5 * jnp.maximum(0.0, 1.0 - col8 / width) * has_left
     ramp_right = 0.5 * jnp.maximum(0.0, 1.0 - (1023.0 - col8) / width) * has_right
+    base = []
+    for ch in range(3):
+        tile = values[ch * 8:(ch + 1) * 8]
+        result = tile - top * tile[0:1] - bottom * tile[7:8]
+        if nz > 1:
+            result = result - ramp_left * tile[:, 0:1] - ramp_right * tile[:, 1023:]
+        base.append(result)
+    for copy in halo:
+        copy.wait_recv()
     up, down = opened(0), opened(1)
     for ch in range(3):
-        tile = values[ch * 8:(ch + 1) * 8]
-        result = tile + top * (up[ch] - tile[0:1]) + bottom * (down[ch] - tile[7:8])
+        result = base[ch] + top * up[ch] + bottom * down[ch]
         if nz > 1:
             left_col = srecv[0, ch * 8:(ch + 1) * 8, 127:128].astype(F32)
             right_col = srecv[1, ch * 8:(ch + 1) * 8, 0:1].astype(F32)
-            result = result + ramp_left * (left_col - tile[:, 0:1]) + ramp_right * (right_col - tile[:, 1023:])
+            result = result + ramp_left * left_col + ramp_right * right_col
         out[ch] = result.astype(BF16)
 
     for r in range(1, PEERS):
@@ -307,7 +306,7 @@
             copy_chunk(k, r).wait_send()
     for rel in range(1, NY):
         copy_weight(rel).wait_send()
-    for slot in range(NY):
+    for slot in range(1, NY):
         copy_sum(slot).wait_send()
     for copy in halo:
         copy.wait_send()
@@ -317,6 +316,13 @@
     frames, col_start, col_weights, footprint, row_start, row_weights, seg_weight, feather_width
 ):
     nz = lax.axis_size("across")
+    held = [
+        pltpu.with_memory_space_constraint(value, pltpu.HBM)
+        for value in (
+            frames, col_start, col_weights, footprint, jnp.transpose(row_start, (0, 2, 1)),
+            jnp.transpose(row_weights, (0, 2, 3, 1)), seg_weight,
+        )
+    ]
     vmem = pl.BlockSpec(memory_space=pltpu.VMEM)
     dma = pltpu.SemaphoreType.DMA
     return pl.pallas_call(
@@ -364,12 +370,9 @@
             dma((4,)),
         ],
         compiler_params=pltpu.CompilerParams(
-            collective_id=0, has_side_effects=True, vmem_limit_bytes=60 * 2**20
+            collective_id=0, has_side_effects=True, vmem_limit_bytes=48 * 2**20
         ),
-    )(
-        frames, col_start, col_weights, footprint, jnp.transpose(row_start, (0, 2, 1)),
-        jnp.transpose(row_weights, (0, 2, 3, 1)), seg_weight, feather_width,
-    )
+    )(*held, feather_width)
 
 
 def solution(mesh):

time: 38.9 us -> 37.5 us (0.964)
  local copies, waits for them, and re-layouts: 1.42 us -> 0.62 us
  Pallas kernels: 36.6 us -> 36.1 us
    unnamed x1, local copies, waits for them, and re-layouts: 1.42 us -> 0.62 us
    pallas_call x1, Pallas kernels: 36.6 us -> 36.1 us  [body(): pl.pallas_call(functools.partial(kernel, nz), out_shape=jax.ShapeDtypeStr...]
where the time goes in v3:
time: 37.5 us; the launch traced here: 37.4 us
  Pallas kernels  36.1 us (96%)
  between operations  0.66 us (2%)
  local copies, waits for them, and re-layouts  0.62 us (2%)
    pallas_call x1, Pallas kernels, body(): pl.pallas_call(functools.partial(kernel, nz), out_shape=jax.ShapeDtypeStr...  36.1 us

profile of v3, /device:TPU:1, one launch (start us, length us, event | category | flops | bytes accessed | tf_op | source)
XLA Modules:
  0.0 37.4 jit_solution(14410761180061068136)
XLA Ops:
  0.7 36.1 %shard_map.82 = bf16[3,8,1024]{2,1,0:T(8,128)(2,1)S(1)} custom-call(bf16[1,3,528,256]{3,2,1,0:T(8,128)(2,1)} %frames.1, s32[1,1024]{1,0:T(1,128)} %col_start.1, bf16[1,4,1024]{2,1,0:T(4,128)(2,1)} %col_weights.1, s32[1,33]{1,0:T(1,128)} %footprint.1, s32[1,8,33]{2,1,0:T(8,128)} %bitcast.3, bf16[1,4,8,33]{3,2,1,0:T(8,128)(2,1)} %bitcast.2, ...), custom_call_target="tpu_custom_call" | custom-call | tf_op jit(solution)/shard_map/pallas_call | solution.py:328
  36.8 0.6 %copy.11 = bf16[3,8,1024]{2,1,0:T(8,128)(2,1)} copy(bf16[3,8,1024]{2,1,0:T(8,128)(2,1)S(1)} %shard_map.82) | data formatting | bytes 98304

commit v4 on v3

--- a/solution.py
+++ b/solution.py
@@ -12,7 +12,7 @@
 BF16 = jnp.bfloat16
 NX, NY, NC = 4, 8, 2
 PEERS = NX * NC
-CHUNKS = ((5, 3), (4, 2), (6, 1), (7, 0))
+CHUNKS = ((5, 3), (4, 2), (6, 0), (7, 1))
 GROUPS = ((0, 4), (1, 5), (3, 7), (2, 6))
 PLACE = {r: 2 * g + i for g, group in enumerate(GROUPS) for i, r in enumerate(group)}
 
@@ -164,7 +164,7 @@
             device_id=y_peer(rel), device_id_type=MESH,
         )
 
-    order = (2, 6, 1, 3, 5, 7, 4)
+    order = (1, 2, 3, 5, 6, 7, 4)
     params[0] = gather[...].astype(BF16)
     load.wait()
     make_chunk(0)

time: 37.5 us -> 36.9 us (0.984)
  Pallas kernels: 36.1 us -> 35.5 us
    pallas_call x1, Pallas kernels: 36.1 us -> 35.5 us  [body(): pl.pallas_call(functools.partial(kernel, nz), out_shape=jax.ShapeDtypeStr...]
where the time goes in v4:
time: 36.9 us; the launch traced here: 36.8 us
  Pallas kernels  35.5 us (96%)
  between operations  0.66 us (2%)
  local copies, waits for them, and re-layouts  0.62 us (2%)
    pallas_call x1, Pallas kernels, body(): pl.pallas_call(functools.partial(kernel, nz), out_shape=jax.ShapeDtypeStr...  35.5 us

profile of v4, /device:TPU:1, one launch (start us, length us, event | category | flops | bytes accessed | tf_op | source)
XLA Modules:
  0.0 36.8 jit_solution(11224023873256274613)
XLA Ops:
  0.7 35.5 %shard_map.82 = bf16[3,8,1024]{2,1,0:T(8,128)(2,1)S(1)} custom-call(bf16[1,3,528,256]{3,2,1,0:T(8,128)(2,1)} %frames.1, s32[1,1024]{1,0:T(1,128)} %col_start.1, bf16[1,4,1024]{2,1,0:T(4,128)(2,1)} %col_weights.1, s32[1,33]{1,0:T(1,128)} %footprint.1, s32[1,8,33]{2,1,0:T(8,128)} %bitcast.3, bf16[1,4,8,33]{3,2,1,0:T(8,128)(2,1)} %bitcast.2, ...), custom_call_target="tpu_custom_call" | custom-call | tf_op jit(solution)/shard_map/pallas_call | solution.py:328
  36.2 0.6 %copy.11 = bf16[3,8,1024]{2,1,0:T(8,128)(2,1)} copy(bf16[3,8,1024]{2,1,0:T(8,128)(2,1)S(1)} %shard_map.82) | data formatting | bytes 98304

commit v5 on v4

--- a/solution.py
+++ b/solution.py
@@ -164,7 +164,7 @@
             device_id=y_peer(rel), device_id_type=MESH,
         )
 
-    order = (1, 2, 3, 5, 6, 7, 4)
+    order = (5, 6, 7, 1, 2, 3, 4)
     params[0] = gather[...].astype(BF16)
     load.wait()
     make_chunk(0)

time: 36.9 us -> 36.4 us (0.986)
  Pallas kernels: 35.5 us -> 35 us
    pallas_call x1, Pallas kernels: 35.5 us -> 35 us  [body(): pl.pallas_call(functools.partial(kernel, nz), out_shape=jax.ShapeDtypeStr...]
where the time goes in v5:
time: 36.4 us; the launch traced here: 36.3 us
  Pallas kernels  35 us (96%)
  between operations  0.66 us (2%)
  local copies, waits for them, and re-layouts  0.62 us (2%)
    pallas_call x1, Pallas kernels, body(): pl.pallas_call(functools.partial(kernel, nz), out_shape=jax.ShapeDtypeStr...  35 us

profile of v5, /device:TPU:1, one launch (start us, length us, event | category | flops | bytes accessed | tf_op | source)
XLA Modules:
  0.0 36.3 jit_solution(1423654853869820516)
XLA Ops:
  0.7 35.0 %shard_map.82 = bf16[3,8,1024]{2,1,0:T(8,128)(2,1)S(1)} custom-call(bf16[1,3,528,256]{3,2,1,0:T(8,128)(2,1)} %frames.1, s32[1,1024]{1,0:T(1,128)} %col_start.1, bf16[1,4,1024]{2,1,0:T(4,128)(2,1)} %col_weights.1, s32[1,33]{1,0:T(1,128)} %footprint.1, s32[1,8,33]{2,1,0:T(8,128)} %bitcast.3, bf16[1,4,8,33]{3,2,1,0:T(8,128)(2,1)} %bitcast.2, ...), custom_call_target="tpu_custom_call" | custom-call | tf_op jit(solution)/shard_map/pallas_call | solution.py:328
  35.7 0.6 %copy.11 = bf16[3,8,1024]{2,1,0:T(8,128)(2,1)} copy(bf16[3,8,1024]{2,1,0:T(8,128)(2,1)S(1)} %shard_map.82) | data formatting | bytes 98304
